TPU v7x, 128 devices: a whole 4x4x4 slice. The times are simulated.
128 devices in a mesh: cells: 32 (over y, z, core), edges: 4 (over x).
Axes of the slice: x: 4, y: 4, z: 4, core: 2. Of those that a mesh axis runs over, the one named last changes fastest.
Arguments:
- cells_in: bfloat16 [262144, 768], P(('cells', 'edges')), may hold values from -6 to 6
- w_in: bfloat16 [768, 768], replicated, may hold values from -0.21875 to 0.21875
- w_edge: bfloat16 [768, 768], replicated, may hold values from -0.21875 to 0.21875
- w_out: bfloat16 [768, 768], replicated, may hold values from -0.21875 to 0.21875
- cotangent: bfloat16 [262144, 768], P(('cells', 'edges')), may hold values from -6 to 6
- cell_row: int32 [262144], P(('cells', 'edges')), may hold values from 0 to 255
- send_slot: int32 [2, 262144], P(None, ('cells', 'edges')), may hold values from 0 to 127, as said below
- recv_target: int32 [128, 128], P(('cells', 'edges')), may hold values from 0 to 256, as said below
Outputs:
- layer_out: bfloat16 [262144, 768], P(('cells', 'edges'))
- grad_cells: bfloat16 [262144, 768], P(('cells', 'edges'))
- grad_win: float32 [768, 768], replicated
- grad_wedge: float32 [768, 768], replicated
- grad_wout: float32 [768, 768], replicated
Inputs may be any that keep to these rules, and one draw needn't show every extreme that they name: send_slot[k, i] is a slot of the device holding cell i; slot j goes to the device at place j // 32 of that device's group of 4, and every slot that a cell names is live at that owner. recv_target[d, e * 32 + c] is the hyperedge among those device d owns that slot (d % 4) * 32 + c of the device at place e of d's group feeds, or 256 for a slot that carries nothing; live slots of one source to one owner come first, each source has at least one live slot to every owner of its group, and some owner of each group receives 32 live slots from every source of the group. cell_row[i] is the row of cell i among the rows of the device holding it.
All inputs are finite; a program needn't handle non-finite values.
Results may differ from a plain program's by a relative error of at most 0.015.
Values may be sent and summed in bfloat16 or wider, within the bound.
A program may use at most 128 MiB of HBM per device.

v0:
```python
import jax
import jax.numpy as jnp
from jax import lax
from jax.sharding import PartitionSpec as P

ROWS_DEV = 256
HE_DEV = 256


def contract_rows(left, right):
    return lax.dot_general(
        left, right, (((0,), (0,)), ((), ())), preferred_element_type=jnp.float32
    )


def times_transpose(left, right):
    return lax.dot_general(
        left, right, (((1,), (1,)), ((), ())), preferred_element_type=jnp.float32
    )


def gather_edges(target_wide, received):
    return lax.dot_general(
        target_wide,
        received,
        (((0,), (0,)), ((), ())),
        precision=lax.Precision.HIGHEST,
        preferred_element_type=jnp.float32,
    )


def per_device(cells_in, w_in, w_edge, w_out, cotangent, cell_row, send_slot, recv_target):
    n_edges = lax.axis_size("edges")
    slots = recv_target.shape[1]
    capacity = slots // n_edges
    width = cells_in.shape[1]
    slot_ids = lax.broadcasted_iota(jnp.int32, (1, slots), 1)
    slot_hot = (send_slot[0][:, None] == slot_ids).astype(jnp.bfloat16) + (
        send_slot[1][:, None] == slot_ids
    ).astype(jnp.bfloat16)
    row_ids = lax.broadcasted_iota(jnp.int32, (1, ROWS_DEV), 1)
    row_hot = (cell_row[:, None] == row_ids).astype(jnp.bfloat16)
    edge_ids = lax.broadcasted_iota(jnp.int32, (1, HE_DEV), 1)
    target_match = recv_target[0][:, None] == edge_ids
    target_wide = target_match.astype(jnp.float32)
    target_narrow = target_match.astype(jnp.bfloat16)
    preact = jnp.dot(cells_in, w_in, preferred_element_type=jnp.float32)
    message = jax.nn.silu(preact).astype(jnp.bfloat16)
    slot_sums = contract_rows(slot_hot, message)
    slot_counts = jnp.sum(slot_hot.astype(jnp.float32), axis=0)
    got_sums, got_counts = (
        lax.all_to_all(
            slot_sums.reshape(n_edges, capacity, width).astype(jnp.bfloat16),
            "edges",
            split_axis=0,
            concat_axis=0,
            tiled=True,
        ).astype(jnp.float32),
        lax.all_to_all(
            slot_counts.reshape(n_edges, capacity).astype(jnp.bfloat16),
            "edges",
            split_axis=0,
            concat_axis=0,
            tiled=True,
        ).astype(jnp.float32),
    )
    edge_sums = gather_edges(target_wide, got_sums.reshape(slots, width))
    edge_counts = jnp.dot(got_counts.reshape(slots), target_wide, precision=lax.Precision.HIGHEST)
    row_sums = contract_rows(row_hot, message)
    row_counts = jnp.sum(row_hot.astype(jnp.float32), axis=0)
    counts_all = jnp.concatenate([row_counts, edge_counts])
    means = (jnp.concatenate([row_sums, edge_sums], axis=0) / (counts_all + 1.0)[:, None]).astype(
        jnp.bfloat16
    )
    hyper_out = jnp.dot(means, w_edge, preferred_element_type=jnp.float32).astype(jnp.bfloat16)
    reply = jnp.dot(target_narrow, hyper_out[ROWS_DEV:], preferred_element_type=jnp.float32).astype(
        jnp.bfloat16
    )
    returned = lax.all_to_all(
        reply.reshape(n_edges, capacity, width), "edges", split_axis=0, concat_axis=0, tiled=True
    )
    mixed = (
        jnp.dot(row_hot, hyper_out[:ROWS_DEV], preferred_element_type=jnp.float32)
        + jnp.dot(slot_hot, returned.reshape(slots, width), preferred_element_type=jnp.float32)
    ).astype(jnp.bfloat16)
    layer_out = (
        cells_in.astype(jnp.float32) + jnp.dot(mixed, w_out, preferred_element_type=jnp.float32)
    ).astype(jnp.bfloat16)
    grad_mixed = times_transpose(cotangent, w_out).astype(jnp.bfloat16)
    grad_wout = contract_rows(mixed, cotangent)
    slot_grads = contract_rows(slot_hot, grad_mixed)
    got_grads = lax.all_to_all(
        slot_grads.reshape(n_edges, capacity, width).astype(jnp.bfloat16),
        "edges",
        split_axis=0,
        concat_axis=0,
        tiled=True,
    ).astype(jnp.float32)
    edge_grads = gather_edges(target_wide, got_grads.reshape(slots, width))
    row_grads = contract_rows(row_hot, grad_mixed)
    hyper_grads = jnp.concatenate([row_grads, edge_grads], axis=0).astype(jnp.bfloat16)
    grad_wedge = contract_rows(means, hyper_grads)
    grad_means = (times_transpose(hyper_grads, w_edge) / (counts_all + 1.0)[:, None]).astype(
        jnp.bfloat16
    )
    answer = jnp.dot(
        target_narrow, grad_means[ROWS_DEV:], preferred_element_type=jnp.float32
    ).astype(jnp.bfloat16)
    answered = lax.all_to_all(
        answer.reshape(n_edges, capacity, width), "edges", split_axis=0, concat_axis=0, tiled=True
    )
    grad_message = jnp.dot(
        row_hot, grad_means[:ROWS_DEV], preferred_element_type=jnp.float32
    ) + jnp.dot(slot_hot, answered.reshape(slots, width), preferred_element_type=jnp.float32)
    sigma = jax.nn.sigmoid(preact)
    grad_pre = (grad_message * sigma * (1.0 + preact * (1.0 - sigma))).astype(jnp.bfloat16)
    grad_cells = (cotangent.astype(jnp.float32) + times_transpose(grad_pre, w_in)).astype(
        jnp.bfloat16
    )
    grad_win = contract_rows(cells_in, grad_pre)
    summed_win, summed_wedge, summed_wout = lax.psum(
        (grad_win, grad_wedge, grad_wout), ("cells", "edges")
    )
    return (layer_out, grad_cells, summed_win, summed_wedge, summed_wout)


def solution(mesh):
    placed = (
        P(("cells", "edges"), None),
        P(),
        P(),
        P(),
        P(("cells", "edges"), None),
        P(("cells", "edges")),
        P(None, ("cells", "edges")),
        P(("cells", "edges"), None),
    )
    return jax.shard_map(
        per_device,
        mesh=mesh,
        in_specs=placed,
        out_specs=(P(("cells", "edges"), None), P(("cells", "edges"), None), P(), P(), P()),
        check_vma=False,
    )
```

profile of v0, /device:TPU:1, one launch (start us, length us, event | category | flops | bytes accessed | tf_op | source)
XLA Modules:
  0.0 273.3 jit_solution(4017949495651273477)
XLA Ops:
  8.0 1.2 fusion.17
  9.9 4.8 %all-to-all-start.1 = ((bf16[4,1,32]{2,1,0:T(2,128)(2,1)}), bf16[4,1,32]{2,1,0:T(2,128)(2,1)S(1)}, u32[]{:S(2)}, u32[]{:S(2)}) async-start(bf16[4,1,32]{2,1,0:T(2,128)(2,1)} %convert_element_type.103), calls=%async_computation.1 | async-start | bytes 4096 | tf_op jit(solution)/shard_map/all_to_all | solution.py:59
  14.7 4.9 %convolution_convert_fusion = bf16[2048,768]{1,0:T(8,128)(2,1)S(1)} fusion(bf16[2048,768]{1,0:T(8,128)(2,1)} %param.12, bf16[768,768]{1,0:T(8,128)(2,1)} %param.11), kind=kOutput, calls=%fused_computation.6 | convolution fusion | flops 2417491968 | bytes 7471104 | tf_op jit(solution)/shard_map/dot_general | solution.py:17
  19.6 2.2 convolution_convert_fusion.4
  21.8 2.0 fusion.6
  23.9 4.9 %multiply_convert_fusion.1 = (bf16[2048,768]{1,0:T(8,128)(2,1)S(1)}, f32[2048,768]{1,0:T(8,128)}) fusion(bf16[2048,768]{1,0:T(8,128)(2,1)S(1)} %copy-done.8, bf16[768,768]{1,0:T(8,128)(2,1)S(1)} %copy-done), kind=kOutput, calls=%fused_computation.4 | convolution fusion | flops 2423783424 | bytes 13762560 | tf_op jit(solution)/shard_map/dot_general | solution.py:47
  28.8 2.2 convolution_convert_fusion.6
  31.0 2.2 fusion.4
  33.5 4.2 %all-to-all-start.3 = ((bf16[4,32,768]{2,1,0:T(8,128)(2,1)}), bf16[4,32,768]{2,1,0:T(8,128)(2,1)S(1)}, u32[]{:S(2)}, u32[]{:S(2)}) async-start(bf16[4,32,768]{2,1,0:T(8,128)(2,1)} %bitcast.8), calls=%async_computation.3 | async-start | bytes 393216 | tf_op jit(solution)/shard_map/all_to_all | solution.py:92
  38.1 4.9 %all-to-all-done.3 = bf16[4,32,768]{2,1,0:T(8,128)(2,1)S(1)} async-done(((bf16[4,32,768]{2,1,0:T(8,128)(2,1)}), bf16[4,32,768]{2,1,0:T(8,128)(2,1)S(1)}, u32[]{:S(2)}, u32[]{:S(2)}) %all-to-all-start.3) | async-done | bytes 196640 | tf_op jit(solution)/shard_map/all_to_all | solution.py:92
  43.0 3.5 %all-to-all-start = ((bf16[4,32,768]{2,1,0:T(8,128)(2,1)}), bf16[4,32,768]{2,1,0:T(8,128)(2,1)S(1)}, u32[]{:S(2)}, u32[]{:S(2)}) async-start(bf16[4,32,768]{2,1,0:T(8,128)(2,1)} %bitcast.3), calls=%async_computation | async-start | bytes 393216 | tf_op jit(solution)/shard_map/all_to_all | solution.py:52
  46.9 1.8 divide_convert_fusion
  48.7 3.2 %fusion = f32[2048,768]{1,0:T(8,128)} fusion(s32[2048]{0:T(1024)S(1)} %copy-done.5, bf16[512,768]{1,0:T(8,128)(2,1)S(1)} %divide_convert_fusion), kind=kOutput, calls=%fused_computation.9 | convolution fusion | flops 805830656 | bytes 6692864 | tf_op jit(solution)/shard_map/dot_general | solution.py:112
  53.3 2.2 convolution_convert_fusion.1
  55.5 2.3 fusion.27
  57.8 4.0 %all-to-all-start.4 = ((bf16[4,32,768]{2,1,0:T(8,128)(2,1)}), bf16[4,32,768]{2,1,0:T(8,128)(2,1)S(1)}, u32[]{:S(2)}, u32[]{:S(2)}) async-start(bf16[4,32,768]{2,1,0:T(8,128)(2,1)} %bitcast.10), calls=%async_computation.4 | async-start | bytes 393216 | tf_op jit(solution)/shard_map/all_to_all | solution.py:109
  61.8 3.3 %fusion.2 = f32[2048,768]{1,0:T(8,128)} fusion(s32[2048]{0:T(1024)S(1)} %copy-done.5, bf16[512,768]{1,0:T(8,128)(2,1)S(1)} %convolution_convert_fusion.1), kind=kOutput, calls=%fused_computation.11 | convolution fusion | flops 805830656 | bytes 6692864 | tf_op jit(solution)/shard_map/dot_general | solution.py:83
  66.0 1.0 all-to-all-done.4
  67.0 3.4 %all-to-all-start.2 = ((bf16[4,32,768]{2,1,0:T(8,128)(2,1)}), bf16[4,32,768]{2,1,0:T(8,128)(2,1)S(1)}, u32[]{:S(2)}, u32[]{:S(2)}) async-start(bf16[4,32,768]{2,1,0:T(8,128)(2,1)} %bitcast.6), calls=%async_computation.2 | async-start | bytes 393216 | tf_op jit(solution)/shard_map/all_to_all | solution.py:79
  70.4 6.8 %multiply_convert_fusion = bf16[2048,768]{1,0:T(8,128)(2,1)S(1)} fusion(f32[2048,768]{1,0:T(8,128)} %get-tuple-element.31, f32[2048,768]{1,0:T(8,128)} %fusion, bf16[128,768]{1,0:T(8,128)(2,1)S(1)} %bitcast.50, s32[2048]{0:T(1024)S(1)} %bitcast.48, s32[2048]{0:T(1024)S(1)} %bitcast.43), kind=kOutput, calls=%fused_computation.1 | convolution fusion | flops 420478976 | bytes 15941632 | tf_op jit(solution)/shard_map/dot_general | solution.py:114
  77.3 1.7 copy-done.13
  79.0 4.1 %convolution_bitcast_fusion = f32[768,768]{0,1:T(8,128)} fusion(bf16[2048,768]{1,0:T(8,128)(2,1)S(1)} %multiply_convert_fusion, bf16[2048,768]{1,0:T(8,128)(2,1)S(1)} %copy-done.9), kind=kOutput, calls=%fused_computation.14 | convolution fusion | flops 2415919104 | bytes 8650752 | tf_op jit(solution)/shard_map/dot_general | solution.py:11
  83.1 3.7 %add_convert_fusion.2 = bf16[2048,768]{1,0:T(8,128)(2,1)S(1)} fusion(f32[2048,768]{1,0:T(8,128)} %fusion.2, bf16[128,768]{1,0:T(8,128)(2,1)S(1)} %bitcast.39, s32[2048]{0:T(1024)S(1)} %bitcast.49, s32[2048]{0:T(1024)S(1)} %bitcast.44), kind=kOutput, calls=%fused_computation.3 | convolution fusion | flops 407896064 | bytes 9650176 | tf_op jit(solution)/shard_map/dot_general | solution.py:84
  86.9 1.7 copy-done.1
  88.6 4.1 %fusion.44 = f32[768,768]{1,0:T(8,128)} fusion(bf16[2048,768]{1,0:T(8,128)(2,1)S(1)} %add_convert_fusion.2, bf16[2048,768]{1,0:T(8,128)(2,1)S(1)} %copy-done.7), kind=kOutput, calls=%fused_computation.61 | convolution fusion | flops 2415919104 | bytes 8650752 | tf_op jit(solution)/shard_map/dot_general | solution.py:11
  92.7 7.3 %add_convert_fusion = bf16[2048,768]{1,0:T(8,128)(2,1)} fusion(bf16[2048,768]{1,0:T(8,128)(2,1)} %param.12, bf16[2048,768]{1,0:T(8,128)(2,1)} %copy-done.13, bf16[768,768]{1,0:T(8,128)(2,1)S(1)} %copy-done), kind=kOutput, calls=%fused_computation | convolution fusion | flops 2420637696 | bytes 10616832 | tf_op jit(solution)/shard_map/dot_general | solution.py:17
  100.1 4.0 %add_convert_fusion.1 = bf16[2048,768]{1,0:T(8,128)(2,1)} fusion(bf16[2048,768]{1,0:T(8,128)(2,1)S(1)} %copy-done.10, bf16[2048,768]{1,0:T(8,128)(2,1)S(1)} %copy-done.2, bf16[768,768]{1,0:T(8,128)(2,1)S(1)} %copy-done.12), kind=kOutput, calls=%fused_computation.2 | convolution fusion | flops 2420637696 | bytes 10616832 | tf_op jit(solution)/shard_map/dot_general | solution.py:87
  104.0 155.3 %all-reduce.3.cloned.1.call-done = (f32[768,768]{0,1:T(8,128)}, f32[768,768]{1,0:T(8,128)}, f32[768,768]{1,0:T(8,128)}) async-done(((f32[768,768]{0,1:T(8,128)}, f32[768,768]{1,0:T(8,128)}, f32[768,768]{1,0:T(8,128)}), (f32[768,768]{0,1:T(8,128)}, f32[768,768]{1,0:T(8,128)}, f32[768,768]{1,0:T(8,128)})) %all-reduce.3.cloned.1.call-update) | async-done | bytes 7077904 | tf_op jit(solution)/shard_map/psum | solution.py:121
  259.4 3.2 %copy.19 = f32[768,768]{1,0:T(8,128)} copy(f32[768,768]{0,1:T(8,128)} %get-tuple-element.25) | data formatting | bytes 4718592
  262.6 1.4 copy.23
  264.0 1.1 copy-done.3
  265.1 1.4 copy.24
  (45 shorter events, 4.9 us)
Async XLA Ops:
  7.2 16.7 %copy-start = (bf16[768,768]{1,0:T(8,128)(2,1)S(1)}, bf16[768,768]{1,0:T(8,128)(2,1)}, u32[]{:S(2)}) copy-start(bf16[768,768]{1,0:T(8,128)(2,1)} %param.9) | copy-start | bytes 3538948
  9.9 23.6 %all-to-all-start.1 = ((bf16[4,1,32]{2,1,0:T(2,128)(2,1)}), bf16[4,1,32]{2,1,0:T(2,128)(2,1)S(1)}, u32[]{:S(2)}, u32[]{:S(2)}) async-start(bf16[4,1,32]{2,1,0:T(2,128)(2,1)} %convert_element_type.103), calls=%async_computation.1 | async-start | bytes 4096 | tf_op jit(solution)/shard_map/all_to_all | solution.py:59
  19.6 2.2 copy-start.5
  21.8 2.0 copy-start.8
  31.0 6.9 %copy-start.6 = (s32[1,128]{1,0:T(1,128)S(1)}, s32[1,128]{1,0:T(1,128)}, u32[]{:S(2)}) copy-start(s32[1,128]{1,0:T(1,128)} %param.15) | copy-start | bytes 1540
  31.0 15.9 %copy-start.11 = (bf16[768,768]{1,0:T(8,128)(2,1)S(1)}, bf16[768,768]{1,0:T(8,128)(2,1)}, u32[]{:S(2)}) copy-start(bf16[768,768]{1,0:T(8,128)(2,1)} %param.10) | copy-start | bytes 3538948
  33.5 9.4 %all-to-all-start.3 = ((bf16[4,32,768]{2,1,0:T(8,128)(2,1)}), bf16[4,32,768]{2,1,0:T(8,128)(2,1)S(1)}, u32[]{:S(2)}, u32[]{:S(2)}) async-start(bf16[4,32,768]{2,1,0:T(8,128)(2,1)} %bitcast.8), calls=%async_computation.3 | async-start | bytes 393216 | tf_op jit(solution)/shard_map/all_to_all | solution.py:92
  43.0 9.9 %all-to-all-start = ((bf16[4,32,768]{2,1,0:T(8,128)(2,1)}), bf16[4,32,768]{2,1,0:T(8,128)(2,1)S(1)}, u32[]{:S(2)}, u32[]{:S(2)}) async-start(bf16[4,32,768]{2,1,0:T(8,128)(2,1)} %bitcast.3), calls=%async_computation | async-start | bytes 393216 | tf_op jit(solution)/shard_map/all_to_all | solution.py:52
  48.7 4.6 %copy-start.14 = (f32[256,768]{1,0:T(8,128)S(1)}, f32[256,768]{1,0:T(8,128)}, u32[]{:S(2)}) copy-start(f32[256,768]{1,0:T(8,128)} %fusion.4) | copy-start | bytes 2359300
  53.3 2.2 copy-start.15
  57.8 9.2 %all-to-all-start.4 = ((bf16[4,32,768]{2,1,0:T(8,128)(2,1)}), bf16[4,32,768]{2,1,0:T(8,128)(2,1)S(1)}, u32[]{:S(2)}, u32[]{:S(2)}) async-start(bf16[4,32,768]{2,1,0:T(8,128)(2,1)} %bitcast.10), calls=%async_computation.4 | async-start | bytes 393216 | tf_op jit(solution)/shard_map/all_to_all | solution.py:109
  67.0 16.1 %all-to-all-start.2 = ((bf16[4,32,768]{2,1,0:T(8,128)(2,1)}), bf16[4,32,768]{2,1,0:T(8,128)(2,1)S(1)}, u32[]{:S(2)}, u32[]{:S(2)}) async-start(bf16[4,32,768]{2,1,0:T(8,128)(2,1)} %bitcast.6), calls=%async_computation.2 | async-start | bytes 393216 | tf_op jit(solution)/shard_map/all_to_all | solution.py:79
  70.4 189.0 %all-reduce.3.cloned.1.call-start = ((), (), s32[]{:S(2)}) async-start(), calls=%async_computation.5 | async-start | bytes 14155776 | tf_op jit(solution)/shard_map/psum | solution.py:121
  70.4 8.6 %copy-start.9 = (bf16[2048,768]{1,0:T(8,128)(2,1)S(1)}, bf16[2048,768]{1,0:T(8,128)(2,1)}, u32[]{:S(2)}) copy-start(bf16[2048,768]{1,0:T(8,128)(2,1)} %param.8) | copy-start | bytes 9437188
  77.3 1.7 copy-start.13
  83.1 5.4 %copy-start.7 = (bf16[2048,768]{1,0:T(8,128)(2,1)S(1)}, bf16[2048,768]{1,0:T(8,128)(2,1)}, u32[]{:S(2)}) copy-start(bf16[2048,768]{1,0:T(8,128)(2,1)} %param.12) | copy-start | bytes 9437188
  86.9 1.7 copy-start.1
  92.7 7.3 %copy-start.2 = (bf16[2048,768]{1,0:T(8,128)(2,1)S(1)}, bf16[2048,768]{1,0:T(8,128)(2,1)}, u32[]{:S(2)}) copy-start(bf16[2048,768]{1,0:T(8,128)(2,1)} %copy-done.1) | copy-start | bytes 9437188
  92.7 7.3 %copy-start.10 = (bf16[2048,768]{1,0:T(8,128)(2,1)S(1)}, bf16[2048,768]{1,0:T(8,128)(2,1)}, u32[]{:S(2)}) copy-start(bf16[2048,768]{1,0:T(8,128)(2,1)} %param.8) | copy-start | bytes 9437188
  92.7 7.3 %copy-start.12 = (bf16[768,768]{1,0:T(8,128)(2,1)S(1)}, bf16[768,768]{1,0:T(8,128)(2,1)}, u32[]{:S(2)}) copy-start(bf16[768,768]{1,0:T(8,128)(2,1)} %param.11) | copy-start | bytes 3538948
  259.4 3.2 %copy-start.4 = (f32[768,768]{1,0:T(8,128)S(1)}, f32[768,768]{1,0:T(8,128)}, u32[]{:S(2)}) copy-start(f32[768,768]{1,0:T(8,128)} %get-tuple-element.35) | copy-start | bytes 7077892
  262.6 2.5 copy-start.3
Sparse Core Ops, SparseCore 0:
  92.8 166.5 all-reduce.2
where the time goes:
time: 274 us; the launch traced here: 273 us
  waiting for transfers between devices  161 us (59%)
  matrix products  64.1 us (23%)
  starting transfers between devices  20.1 us (7%)
  between operations  14.2 us (5%)
  local copies, waits for them, and re-layouts  12.2 us (4%)
    psum x1, waiting for transfers between devices, per_device(): lax.psum((grad_win, grad_wedge, grad_wout), ('cells', 'edges'))  155 us
    dot_general x7, matrix products, contract_rows(): lax.dot_general(left, right, (((0,), (0,)), ((), ())), preferred_element_...  19.2 us
    dot_general x3, matrix products, times_transpose(): lax.dot_general(left, right, (((1,), (1,)), ((), ())), preferred_element_...  14 us
    unnamed x35, local copies, waits for them, and re-layouts  10.6 us
    dot_general x1, matrix products, per_device(): jnp.dot(slot_hot, answered.reshape(slots, width), preferred_element_type=...  6.85 us
  transfers between devices with their start and end apart: 6, of which 3 were waited for; matrix products, arithmetic and copies ran while one was open for 19% of the time, Pallas kernels for 0%

commit v1 on v0

v1 whole, which is shorter than its diff:
```python
import jax
import jax.numpy as jnp
from jax import lax
from jax.experimental import pallas as pl
from jax.experimental.pallas import tpu as pltpu
from jax.sharding import PartitionSpec as P

N = 2048
D = 768
R = 256
H = 256
S = 128
CAP = 32
K = R + S
M = 1024
HALF = D // 2
RA = D // 4
RB = RA // 4
WEDGE, WOUT, WIN = 0, 1, 2

f32 = jnp.float32
bf16 = jnp.bfloat16
NT = (((1,), (1,)), ((), ()))
TN = (((0,), (0,)), ((), ()))


def dot(a, b):
    return jnp.dot(a, b, preferred_element_type=f32)


def dot_nt(a, b):
    return lax.dot_general(a, b, NT, preferred_element_type=f32)


def dot_tn(a, b):
    return lax.dot_general(a, b, TN, preferred_element_type=f32)


def aligned(x, m):
    return pl.multiple_of(x, m)


def kernel(
    cells_h, w_in_h, w_edge_h, w_out_h, cot_h, row_ref, slot_ref, tgt_ref,
    lo_h, gc_h, fin_h,
    cells, cot, w_in, w_edge, w_out, dact, msg, gmix, hot_t, hot, ids,
    means, hgrads, hout, gmean, tgt_t, inv,
    out1, out3, got1, got3, reply2, reply4, cat2, cat4,
    send0, recv0, part, send_a, recv_a, part_b, send_b, recv_b, recv_c, fin,
    in_sem, lo_sem, gc_sem, fin_sem,
    x_ss, x_rs, p_ss, p_rs, a_ss, a_rs, b_ss, b_rs, c_ss, c_rs,
    bg_ss, bg_rs, ag_ss, ag_rs, pg_ss, pg_rs,
):
    ci = lax.axis_index("cells")
    x = lax.axis_index("edges")
    core = lax.rem(ci, 2)
    z = lax.rem(lax.div(ci, 2), 4)
    y = lax.div(ci, 8)

    def on_x(k):
        return {"cells": ci, "edges": lax.rem(x + k, 4)}

    def on_y(k):
        return {"cells": (lax.rem(y + k, 4) * 4 + z) * 2 + core, "edges": x}

    def on_z(k):
        return {"cells": (y * 4 + lax.rem(z + k, 4)) * 2 + core, "edges": x}

    twin = {"cells": ci + 1 - 2 * core, "edges": x}
    at = (x, y, z)
    peer = (on_x, on_y, on_z)

    loads = {}

    def load(name, src, dst, i):
        loads[name] = pltpu.make_async_copy(src, dst, in_sem.at[i])
        loads[name].start()

    load("w_in", w_in_h, w_in, 0)
    load("cells0", cells_h.at[pl.ds(0, M)], cells.at[pl.ds(0, M)], 1)
    load("cells1", cells_h.at[pl.ds(M, M)], cells.at[pl.ds(M, M)], 2)
    load("w_out", w_out_h, w_out, 3)
    load("cot0", cot_h.at[pl.ds(0, M)], cot.at[pl.ds(0, M)], 4)
    load("cot1", cot_h.at[pl.ds(M, M)], cot.at[pl.ds(M, M)], 5)
    load("w_edge", w_edge_h, w_edge, 6)

    barrier = pltpu.get_barrier_semaphore()
    for k in (1, 2, 3):
        for where in peer:
            pl.semaphore_signal(
                barrier, inc=1, device_id=where(k), device_id_type=pl.DeviceIdType.MESH
            )
    pl.semaphore_signal(barrier, inc=1, device_id=twin, device_id_type=pl.DeviceIdType.MESH)

    started = []

    def send(src, dst, ss, rs, where):
        copy = pltpu.make_async_remote_copy(
            src_ref=src, dst_ref=dst, send_sem=ss, recv_sem=rs,
            device_id=where, device_id_type=pl.DeviceIdType.MESH,
        )
        copy.start()
        started.append(copy)
        return copy

    ids[...] = jnp.zeros_like(ids)
    ids[0:1, :] = row_ref[...]
    ids[1:3, :] = slot_ref[...]
    tgt_t[...] = (lax.broadcasted_iota(jnp.int32, (H, S), 0) == tgt_ref[...]).astype(bf16)

    def ones_where(mask):
        return jnp.where(mask, 1.0, 0.0)

    for i in range(N // M):
        rows = pl.ds(i * M, M)
        if i == 0:
            loads["w_in"].wait()
        loads["cells%d" % i].wait()
        pre = dot(cells[rows, :], w_in[...])
        sig = 0.5 * jnp.tanh(0.5 * pre) + 0.5
        m = pre * sig
        msg[rows, :] = m.astype(bf16)
        dact[rows, :] = (sig + m * (1.0 - sig)).astype(bf16)
        some = ids[:, rows]
        hot_t[0:R, rows] = ones_where(
            lax.broadcasted_iota(jnp.int32, (R, M), 0) == some[0:1, :]
        ).astype(bf16)
        slot_i = lax.broadcasted_iota(jnp.int32, (S, M), 0)
        hot_t[R:K, rows] = (
            ones_where(slot_i == some[1:2, :]) + ones_where(slot_i == some[2:3, :])
        ).astype(bf16)
        col = some.T
        hot[rows, 0:R] = ones_where(
            lax.broadcasted_iota(jnp.int32, (M, R), 1) == col[:, 0:1]
        ).astype(bf16)
        slot_j = lax.broadcasted_iota(jnp.int32, (M, S), 1)
        hot[rows, R:K] = (
            ones_where(slot_j == col[:, 1:2]) + ones_where(slot_j == col[:, 2:3])
        ).astype(bf16)

    ones = jnp.ones((N, S), bf16)
    out1[:, 0:D] = dot(hot_t[R:K, :], msg[...]).astype(bf16)
    count = dot(hot_t[R:K, :], ones)
    high = jnp.floor(count * (1.0 / 128.0)) * 128.0
    lane = lax.broadcasted_iota(jnp.int32, (S, S), 1)
    out1[:, D:] = jnp.where(lane < S // 2, high, count - high).astype(bf16)

    pl.semaphore_wait(barrier, 10)

    def exchange(kind, src, dst, base):
        mine = pl.ds(aligned(base + x * CAP, CAP), CAP)
        copies = []
        for k in (1, 2, 3):
            theirs = pl.ds(aligned(lax.rem(x + k, 4) * CAP, CAP), CAP)
            copies.append(
                send(src.at[theirs], dst.at[mine], x_ss.at[kind, k - 1], x_rs.at[kind, k - 1], on_x(k))
            )
        dst[mine, :] = src[pl.ds(aligned(x * CAP, CAP), CAP), :]
        return copies

    x1 = exchange(0, out1, got1, 0)

    loads["w_out"].wait()
    for i in range(N // M):
        rows = pl.ds(i * M, M)
        loads["cot%d" % i].wait()
        gmix[rows, :] = dot_nt(cot[rows, :], w_out[...]).astype(bf16)
    out3[...] = dot(hot_t[R:K, :], gmix[...]).astype(bf16)
    x3 = exchange(1, out3, got3, 0)

    loads["w_edge"].wait()
    inv[0:R, :] = 1.0 / (dot(hot_t[0:R, :], ones) + 1.0)
    means[0:R, :] = (dot(hot_t[0:R, :], msg[...]) * inv[0:R, 0:1]).astype(bf16)
    for copy in x1:
        copy.wait_recv()
    counted = dot(tgt_t[...], got1[:, D:])
    inv[R:, :] = jnp.broadcast_to(
        1.0 / (counted[:, 0:1] + counted[:, S // 2 : S // 2 + 1] + 1.0), (H, S)
    )
    means[R:, :] = (dot(tgt_t[...], got1[:, 0:D]) * inv[R:, 0:1]).astype(bf16)
    hout[...] = dot(means[R:, :], w_edge[...]).astype(bf16)
    reply2[...] = dot_tn(tgt_t[...], hout[...]).astype(bf16)
    x2 = exchange(2, reply2, cat2, R)
    cat2[0:R, :] = dot(means[0:R, :], w_edge[...]).astype(bf16)
    hgrads[0:R, :] = dot(hot_t[0:R, :], gmix[...]).astype(bf16)
    for copy in x3:
        copy.wait_recv()
    hgrads[R:, :] = dot(tgt_t[...], got3[...]).astype(bf16)
    gmean[...] = (dot_nt(hgrads[R:, :], w_edge[...]) * inv[R:, 0:1]).astype(bf16)
    reply4[...] = dot_tn(tgt_t[...], gmean[...]).astype(bf16)
    x4 = exchange(3, reply4, cat4, R)
    cat4[0:R, :] = (dot_nt(hgrads[0:R, :], w_edge[...]) * inv[0:R, 0:1]).astype(bf16)

    near = pl.ds(aligned(core * HALF, 128), HALF)
    far = pl.ds(aligned((1 - core) * HALF, 128), HALF)
    axes = ((0, 1, 2), (1, 2, 0), (2, 0, 1))
    held = {}

    def gradient(g, left, right):
        send0[g] = dot_tn(left[...], right[:, far]).astype(bf16)
        held[g, "p"] = send(send0.at[g], recv0.at[g], p_ss.at[g], p_rs.at[g], twin)
        part[g] = dot_tn(left[...], right[:, near])

    def step_a(g):
        held[g, "p"].wait_recv()
        total = part[g] + recv0[g].astype(f32)
        part[g] = total
        send_a[g] = total.astype(bf16)
        for t in range(3):
            ax = axes[t][0]
            for k in (1, 2, 3):
                theirs = pl.ds(aligned(lax.rem(at[ax] + k, 4) * RA, RA), RA)
                held[g, "a", t, k] = send(
                    send_a.at[g, theirs, pl.ds(t * 128, 128)], recv_a.at[g, k - 1, t],
                    a_ss.at[g, t, k - 1], a_rs.at[g, t, k - 1], peer[ax](k),
                )

    def step_b(g):
        for t in range(3):
            ax = axes[t][1]
            mine = pl.ds(aligned(at[axes[t][0]] * RA, RA), RA)
            total = part[g, mine, t * 128 : (t + 1) * 128]
            for k in (1, 2, 3):
                held[g, "a", t, k].wait_recv()
                total = total + recv_a[g, k - 1, t].astype(f32)
            part_b[g, t] = total
            send_b[g, t] = total.astype(bf16)
            for k in (1, 2, 3):
                theirs = pl.ds(aligned(lax.rem(at[ax] + k, 4) * RB, RB), RB)
                held[g, "b", t, k] = send(
                    send_b.at[g, t, theirs], recv_b.at[g, k - 1, t],
                    b_ss.at[g, t, k - 1], b_rs.at[g, t, k - 1], peer[ax](k),
                )

    def step_c(g):
        for t in range(3):
            ax = axes[t][2]
            mine = pl.ds(aligned(at[axes[t][1]] * RB, RB), RB)
            total = part_b[g, t, mine, :]
            for k in (1, 2, 3):
                held[g, "b", t, k].wait_recv()
                total = total + recv_b[g, k - 1, t].astype(f32)
            recv_c[g, t, pl.ds(at[ax], 1)] = total.astype(bf16)[None]
            for k in (1, 2, 3):
                held[g, "c", t, k] = send(
                    recv_c.at[g, t, at[ax]], recv_c.at[g, t, at[ax]],
                    c_ss.at[g, t, k - 1], c_rs.at[g, t, k - 1], peer[ax](k),
                )

    def column(t):
        return pl.ds(aligned(core * HALF + t * 128, 128), 128)

    def gather_b(g):
        for t in range(3):
            ax = axes[t][1]
            for k in (1, 2, 3):
                held[g, "c", t, k].wait_recv()
            total = recv_c[g, t, 0].astype(f32)
            for k in (1, 2, 3):
                total = total + recv_c[g, t, k].astype(f32)
            place = pl.ds(aligned(at[axes[t][0]] * RA + at[ax] * RB, RB), RB)
            fin[g, place, column(t)] = total.astype(bf16)
            block = fin.at[g, place, column(t)]
            for k in (1, 2, 3):
                held[g, "bg", t, k] = send(
                    block, block, bg_ss.at[g, t, k - 1], bg_rs.at[g, t, k - 1], peer[ax](k)
                )

    def gather_a(g):
        for t in range(3):
            ax = axes[t][0]
            for k in (1, 2, 3):
                held[g, "bg", t, k].wait_recv()
            block = fin.at[g, pl.ds(aligned(at[ax] * RA, RA), RA), column(t)]
            for k in (1, 2, 3):
                held[g, "ag", t, k] = send(
                    block, block, ag_ss.at[g, t, k - 1], ag_rs.at[g, t, k - 1], peer[ax](k)
                )

    def gather_p(g):
        for t in range(3):
            for k in (1, 2, 3):
                held[g, "ag", t, k].wait_recv()
            block = fin.at[g, :, column(t)]
            held[g, "pg", t] = send(block, block, pg_ss.at[g, t], pg_rs.at[g, t], twin)

    def finish(g):
        for t in range(3):
            held[g, "pg", t].wait_recv()
        done = pltpu.make_async_copy(fin.at[g], fin_h.at[g], fin_sem.at[g])
        done.start()
        return done

    gradient(WEDGE, means, hgrads)

    mixed = msg
    for copy in x2:
        copy.wait_recv()
    for i in range(N // M):
        rows = pl.ds(i * M, M)
        mixed[rows, :] = dot(hot[rows, :], cat2[...]).astype(bf16)
    step_a(WEDGE)
    gradient(WOUT, mixed, cot)
    step_b(WEDGE)
    gpre = gmix
    for copy in x4:
        copy.wait_recv()
    for i in range(N // M):
        rows = pl.ds(i * M, M)
        gpre[rows, :] = (dot(hot[rows, :], cat4[...]) * dact[rows, :].astype(f32)).astype(bf16)
    step_a(WOUT)
    step_c(WEDGE)
    gradient(WIN, cells, gpre)
    gather_b(WEDGE)
    step_a(WIN)
    step_b(WOUT)

    stores = []

    def layer_out(i):
        rows = pl.ds(i * M, M)
        mixed[rows, :] = (cells[rows, :].astype(f32) + dot(mixed[rows, :], w_out[...])).astype(bf16)
        done = pltpu.make_async_copy(mixed.at[rows], lo_h.at[rows], lo_sem.at[i])
        done.start()
        stores.append(done)

    def grad_cells(i):
        rows = pl.ds(i * M, M)
        gpre[rows, :] = (cot[rows, :].astype(f32) + dot_nt(gpre[rows, :], w_in[...])).astype(bf16)
        done = pltpu.make_async_copy(gpre.at[rows], gc_h.at[rows], gc_sem.at[i])
        done.start()
        stores.append(done)

    layer_out(0)
    gather_a(WEDGE)
    step_c(WOUT)
    step_b(WIN)
    layer_out(1)
    gather_b(WOUT)
    step_c(WIN)
    gather_p(WEDGE)
    grad_cells(0)
    gather_a(WOUT)
    gather_b(WIN)
    stores.append(finish(WEDGE))
    grad_cells(1)
    gather_a(WIN)
    gather_p(WOUT)
    stores.append(finish(WOUT))
    gather_p(WIN)
    stores.append(finish(WIN))
    for done in stores:
        done.wait()
    for copy in started:
        copy.wait_send()


def per_device(cells_in, w_in, w_edge, w_out, cotangent, cell_row, send_slot, recv_target):
    any_spec = pl.BlockSpec(memory_space=pl.ANY)
    vmem = pl.BlockSpec(memory_space=pltpu.VMEM)
    dma = pltpu.SemaphoreType.DMA
    scratch = [
        pltpu.VMEM((N, D), bf16),
        pltpu.VMEM((N, D), bf16),
        pltpu.VMEM((D, D), bf16),
        pltpu.VMEM((D, D), bf16),
        pltpu.VMEM((D, D), bf16),
        pltpu.VMEM((N, D), bf16),
        pltpu.VMEM((N, D), bf16),
        pltpu.VMEM((N, D), bf16),
        pltpu.VMEM((K, N), bf16),
        pltpu.VMEM((N, K), bf16),
        pltpu.VMEM((8, N), jnp.int32),
        pltpu.VMEM((R + H, D), bf16),
        pltpu.VMEM((R + H, D), bf16),
        pltpu.VMEM((H, D), bf16),
        pltpu.VMEM((H, D), bf16),
        pltpu.VMEM((H, S), bf16),
        pltpu.VMEM((R + H, S), f32),
        pltpu.VMEM((S, D + S), bf16),
        pltpu.VMEM((S, D), bf16),
        pltpu.VMEM((S, D + S), bf16),
        pltpu.VMEM((S, D), bf16),
        pltpu.VMEM((S, D), bf16),
        pltpu.VMEM((S, D), bf16),
        pltpu.VMEM((K, D), bf16),
        pltpu.VMEM((K, D), bf16),
        pltpu.VMEM((3, D, HALF), bf16),
        pltpu.VMEM((3, D, HALF), bf16),
        pltpu.VMEM((3, D, HALF), f32),
        pltpu.VMEM((3, D, HALF), bf16),
        pltpu.VMEM((3, 3, 3, RA, 128), bf16),
        pltpu.VMEM((3, 3, RA, 128), f32),
        pltpu.VMEM((3, 3, RA, 128), bf16),
        pltpu.VMEM((3, 3, 3, RB, 128), bf16),
        pltpu.VMEM((3, 3, 4, RB, 128), bf16),
        pltpu.VMEM((3, D, D), bf16),
        dma((7,)),
        dma((2,)),
        dma((2,)),
        dma((3,)),
        dma((4, 3)),
        dma((4, 3)),
        dma((3,)),
        dma((3,)),
        dma((3, 3, 3)),
        dma((3, 3, 3)),
        dma((3, 3, 3)),
        dma((3, 3, 3)),
        dma((3, 3, 3)),
        dma((3, 3, 3)),
        dma((3, 3, 3)),
        dma((3, 3, 3)),
        dma((3, 3, 3)),
        dma((3, 3, 3)),
        dma((3, 3)),
        dma((3, 3)),
    ]
    layer_out, grad_cells, fin = pl.pallas_call(
        kernel,
        out_shape=(
            jax.ShapeDtypeStruct((N, D), bf16),
            jax.ShapeDtypeStruct((N, D), bf16),
            jax.ShapeDtypeStruct((3, D, D), bf16),
        ),
        in_specs=[any_spec] * 5 + [vmem] * 3,
        out_specs=(any_spec, any_spec, any_spec),
        scratch_shapes=scratch,
        compiler_params=pltpu.CompilerParams(
            collective_id=0, has_side_effects=True, vmem_limit_bytes=56 * 2**20
        ),
        name="layer",
    )(
        cells_in, w_in, w_edge, w_out, cotangent,
        cell_row.reshape(1, N), send_slot, recv_target,
    )
    wide = fin.astype(f32)
    return layer_out, grad_cells, wide[WIN], wide[WEDGE], wide[WOUT]


def solution(mesh):
    placed = (
        P(("cells", "edges"), None),
        P(),
        P(),
        P(),
        P(("cells", "edges"), None),
        P(("cells", "edges")),
        P(None, ("cells", "edges")),
        P(("cells", "edges"), None),
    )
    return jax.shard_map(
        per_device,
        mesh=mesh,
        in_specs=placed,
        out_specs=(P(("cells", "edges"), None), P(("cells", "edges"), None), P(), P(), P()),
        check_vma=False,
    )
```

time: 274 us -> 80.1 us (0.29)
  waiting for transfers between devices: 161 us -> 0 us
  Pallas kernels: 0 us -> 68.1 us
  matrix products: 64.1 us -> 0 us
  starting transfers between devices: 20.1 us -> 0 us
  between operations: 14.2 us -> 0.66 us
  local copies, waits for them, and re-layouts: 12.2 us -> 8.47 us
    psum x1 -> x0, waiting for transfers between devices: 155 us -> none  [per_device(): lax.psum((grad_win, grad_wedge, grad_wout), ('cells', 'edges'))]
    pallas_call x0 -> x1, Pallas kernels: none -> 68.1 us  [per_device(): pl.pallas_call(kernel, out_shape=(jax.ShapeDtypeStruct((N, D), bf16), jax...]
    dot_general x22 -> x0, matrix products: 64.1 us -> none  [the longest x7 19.2 us: contract_rows(): lax.dot_general(left, right, (((0,), (0,)), ((), ())), preferred_element_...]
    all_to_all x5 -> x0, starting transfers between devices: 20 us -> none  [the longest x1 4.84 us: per_device(): lax.all_to_all(slot_counts.reshape(n_edges, capacity).astype(jnp.bfloat16...]
    all_to_all x5 -> x0, waiting for transfers between devices: 5.82 us -> none  [the longest x1 4.85 us: per_device(): lax.all_to_all(slot_grads.reshape(n_edges, capacity, width).astype(jnp.bf...]
    unnamed x35 -> x6, local copies, waits for them, and re-layouts: 10.6 us -> 5.1 us
    squeeze x0 -> x1, local copies, waits for them, and re-layouts: none -> 3.37 us  [per_device(): return (layer_out, grad_cells, wide[WIN], wide[WEDGE], wide[WOUT])]
  transfers between devices with their start and end apart: 6 -> 0, of which waited for: 3 -> 0; matrix products, arithmetic and copies ran while one was open for 19% -> 0% of each run, Pallas kernels for 0% -> 0%
where the time goes in v1:
time: 80.1 us; the launch traced here: 79.8 us
  Pallas kernels  68.1 us (85%)
  local copies, waits for them, and re-layouts  8.47 us (11%)
  other arithmetic  2.6 us (3%)
    pallas_call x1, Pallas kernels, per_device(): pl.pallas_call(kernel, out_shape=(jax.ShapeDtypeStruct((N, D), bf16), jax...  68.1 us
    unnamed x6, local copies, waits for them, and re-layouts  5.1 us
    squeeze x1, local copies, waits for them, and re-layouts, per_device(): return (layer_out, grad_cells, wide[WIN], wide[WEDGE], wide[WOUT])  3.37 us
    convert_element_type x1, other arithmetic, per_device(): wide = fin.astype(f32)  2.6 us

profile of v1, /device:TPU:1, one launch (start us, length us, event | category | flops | bytes accessed | tf_op | source)
XLA Modules:
  0.0 79.8 jit_solution(770190038250003660)
XLA Ops:
  0.6 68.1 %layer.1 = (bf16[2048,768]{1,0:T(8,128)(2,1)}, bf16[2048,768]{1,0:T(8,128)(2,1)}, bf16[3,768,768]{2,1,0:T(8,128)(2,1)}) custom-call(bf16[2048,768]{1,0:T(8,128)(2,1)} %cells_h.1, bf16[768,768]{1,0:T(8,128)(2,1)} %w_in_h.1, bf16[768,768]{1,0:T(8,128)(2,1)} %w_edge_h.1, bf16[768,768]{1,0:T(8,128)(2,1)} %w_out_h.1, bf16[2048,768]{1,0:T(8,128)(2,1)} %cot_h.1, ...), custom_call_target="tpu_custom_call" | custom-call | tf_op jit(solution)/shard_map/layer/pallas_call | solution.py:419
  68.7 2.6 %convert_element_type.3 = f32[3,768,768]{2,1,0:T(8,128)S(1)} convert(bf16[3,768,768]{2,1,0:T(8,128)(2,1)} %get-tuple-element.10) | non-fusion elementwise | flops 1769472 | bytes 10616832 | tf_op jit(solution)/shard_map/convert_element_type | solution.py:437
  71.3 0.0 copy-start.1
  71.3 3.4 %slice_bitcast_fusion = (f32[768,768]{1,0:T(8,128)}, f32[768,768]{1,0:T(8,128)}, f32[768,768]{1,0:T(8,128)}) fusion(f32[3,768,768]{2,1,0:T(8,128)S(1)} %convert_element_type.3), kind=kLoop, calls=%fused_computation | loop fusion | bytes 14155776 | tf_op jit(solution)/shard_map/squeeze | solution.py:438
  74.7 0.4 copy-done.1
  75.1 0.0 copy-start
  75.1 1.7 %copy.15 = bf16[2048,768]{1,0:T(8,128)(2,1)} copy(bf16[2048,768]{1,0:T(8,128)(2,1)S(1)} %copy-done.1) | data formatting | bytes 6291456
  76.8 1.4 %copy-done = bf16[2048,768]{1,0:T(8,128)(2,1)S(1)} copy-done((bf16[2048,768]{1,0:T(8,128)(2,1)S(1)}, bf16[2048,768]{1,0:T(8,128)(2,1)}, u32[]{:S(2)}) %copy-start) | copy-done | bytes 3145752
  78.1 1.7 %copy.16 = bf16[2048,768]{1,0:T(8,128)(2,1)} copy(bf16[2048,768]{1,0:T(8,128)(2,1)S(1)} %copy-done) | data formatting | bytes 6291456
Async XLA Ops:
  71.3 3.8 %copy-start.1 = (bf16[2048,768]{1,0:T(8,128)(2,1)S(1)}, bf16[2048,768]{1,0:T(8,128)(2,1)}, u32[]{:S(2)}) copy-start(bf16[2048,768]{1,0:T(8,128)(2,1)} %get-tuple-element.19) | copy-start | bytes 9437188
  75.1 3.0 %copy-start = (bf16[2048,768]{1,0:T(8,128)(2,1)S(1)}, bf16[2048,768]{1,0:T(8,128)(2,1)}, u32[]{:S(2)}) copy-start(bf16[2048,768]{1,0:T(8,128)(2,1)} %get-tuple-element.20) | copy-start | bytes 9437188

commit v2 on v1

v2 whole, which is shorter than its diff:
```python
import jax
import jax.numpy as jnp
from jax import lax
from jax.experimental import pallas as pl
from jax.experimental.pallas import tpu as pltpu
from jax.sharding import PartitionSpec as P

N = 2048
D = 768
R = 256
H = 256
S = 128
CAP = 32
K = R + S
M = 1024
HALF = D // 2
WEDGE, WOUT, WIN = 0, 1, 2
BOTH = (0, 2)
LAST = (2, 1)

f32 = jnp.float32
bf16 = jnp.bfloat16
NT = (((1,), (1,)), ((), ()))
TN = (((0,), (0,)), ((), ()))


def dot(a, b):
    return jnp.dot(a, b, preferred_element_type=f32)


def dot_nt(a, b):
    return lax.dot_general(a, b, NT, preferred_element_type=f32)


def dot_tn(a, b):
    return lax.dot_general(a, b, TN, preferred_element_type=f32)


def aligned(x, m):
    return pl.multiple_of(x, m)


def kernel(
    cells_h, w_in_h, w_edge_h, w_out_h, cot_h, row_h, slot_h, tgt_h,
    mixed, gpre, win_ref, wedge_ref, wout_ref,
    row_ref, slot_ref, tgt_ref, cells, cot, w_in, w_edge, w_out, dact, hot_t, hot, ids,
    means, hgrads, hout, gmean, tgt_t, inv,
    out1, out3, got1, got3, reply2, reply4, cat2, cat4,
    send0, recv0, part, send_a, recv_a, part_b, send_b, recv_b, recv_c, fin,
    in_sem,
    x_ss, x_rs, p_ss, p_rs, a_ss, a_rs, b_ss, b_rs, c_ss, c_rs,
    bg_ss, bg_rs, ag_ss, ag_rs, pg_ss, pg_rs,
):
    ci = lax.axis_index("cells")
    x = lax.axis_index("edges")
    core = lax.rem(ci, 2)
    z = lax.rem(lax.div(ci, 2), 4)
    y = lax.div(ci, 8)

    def on_x(k):
        return {"cells": ci, "edges": lax.rem(x + k, 4)}

    def on_y(k):
        return {"cells": (lax.rem(y + k, 4) * 4 + z) * 2 + core, "edges": x}

    def on_z(k):
        return {"cells": (y * 4 + lax.rem(z + k, 4)) * 2 + core, "edges": x}

    twin = {"cells": ci + 1 - 2 * core, "edges": x}
    at = (x, y, z)
    peer = (on_x, on_y, on_z)

    msg, gmix = mixed, gpre

    loads = {}

    def arrive(name):
        loads.pop(name).wait()

    def load(name, src, dst, i):
        loads[name] = pltpu.make_async_copy(src, dst, in_sem.at[i])
        loads[name].start()

    for i, (name, src, dst) in enumerate(
        (
            ("rows", row_h, row_ref),
            ("slots", slot_h, slot_ref),
            ("targets", tgt_h, tgt_ref),
            ("w_in", w_in_h, w_in),
            ("cells0", cells_h.at[pl.ds(0, M)], cells.at[pl.ds(0, M)]),
            ("cells1", cells_h.at[pl.ds(M, M)], cells.at[pl.ds(M, M)]),
            ("w_out", w_out_h, w_out),
            ("cot0", cot_h.at[pl.ds(0, M)], cot.at[pl.ds(0, M)]),
            ("cot1", cot_h.at[pl.ds(M, M)], cot.at[pl.ds(M, M)]),
            ("w_edge", w_edge_h, w_edge),
        )
    ):
        load(name, src, dst, i)

    barrier = pltpu.get_barrier_semaphore()
    for k in (1, 2, 3):
        for where in peer:
            pl.semaphore_signal(
                barrier, inc=1, device_id=where(k), device_id_type=pl.DeviceIdType.MESH
            )
    pl.semaphore_signal(barrier, inc=1, device_id=twin, device_id_type=pl.DeviceIdType.MESH)

    sent = []

    def send(src, dst, ss, rs, where):
        pltpu.make_async_remote_copy(
            src_ref=src, dst_ref=dst, send_sem=ss, recv_sem=rs,
            device_id=where, device_id_type=pl.DeviceIdType.MESH,
        ).start()

    def take(ref, sem):
        pltpu.make_async_copy(ref, ref, sem).wait()

    for name in ("rows", "slots", "targets"):
        arrive(name)
    ids[...] = jnp.zeros_like(ids)
    ids[0:1, :] = row_ref[...]
    ids[1:3, :] = slot_ref[...]
    tgt_t[...] = (lax.broadcasted_iota(jnp.int32, (H, S), 0) == tgt_ref[...]).astype(bf16)

    def ones_where(mask):
        return jnp.where(mask, 1.0, 0.0)

    def incidences(i):
        rows = pl.ds(i * M, M)
        some = ids[:, rows]
        hot_t[0:R, rows] = ones_where(
            lax.broadcasted_iota(jnp.int32, (R, M), 0) == some[0:1, :]
        ).astype(bf16)
        slot_i = lax.broadcasted_iota(jnp.int32, (S, M), 0)
        hot_t[R:K, rows] = (
            ones_where(slot_i == some[1:2, :]) + ones_where(slot_i == some[2:3, :])
        ).astype(bf16)
        col = some.T
        hot[rows, 0:R] = ones_where(
            lax.broadcasted_iota(jnp.int32, (M, R), 1) == col[:, 0:1]
        ).astype(bf16)
        slot_j = lax.broadcasted_iota(jnp.int32, (M, S), 1)
        hot[rows, R:K] = (
            ones_where(slot_j == col[:, 1:2]) + ones_where(slot_j == col[:, 2:3])
        ).astype(bf16)

    incidences(0)
    arrive("w_in")
    for i in range(N // M):
        rows = pl.ds(i * M, M)
        arrive("cells%d" % i)
        pre = dot(cells[rows, :], w_in[...])
        sig = 0.5 * jnp.tanh(0.5 * pre) + 0.5
        m = pre * sig
        msg[rows, :] = m.astype(bf16)
        dact[rows, :] = (sig + m * (1.0 - sig)).astype(bf16)
        if i == 0:
            incidences(1)

    ones = jnp.ones((N, S), bf16)
    out1[:, 0:D] = dot(hot_t[R:K, :], msg[...]).astype(bf16)
    count = dot(hot_t[R:K, :], ones)
    high = jnp.floor(count * (1.0 / 128.0)) * 128.0
    lane = lax.broadcasted_iota(jnp.int32, (S, S), 1)
    out1[:, D:] = jnp.where(lane < S // 2, high, count - high).astype(bf16)

    pl.semaphore_wait(barrier, 10)

    def exchange(kind, src, dst, base):
        mine = pl.ds(aligned(base + x * CAP, CAP), CAP)
        for k in (2, 1, 3):
            theirs = pl.ds(aligned(lax.rem(x + k, 4) * CAP, CAP), CAP)
            send(src.at[theirs], dst.at[mine], x_ss.at[kind], x_rs.at[kind], on_x(k))
        sent.append((src.at[pl.ds(0, 3 * CAP)], x_ss.at[kind]))
        dst[mine, :] = src[pl.ds(aligned(x * CAP, CAP), CAP), :]

    def arrived(kind, dst):
        take(dst.at[pl.ds(0, 3 * CAP)], x_rs.at[kind])

    exchange(0, out1, got1, 0)

    arrive("w_out")
    for i in range(N // M):
        rows = pl.ds(i * M, M)
        arrive("cot%d" % i)
        gmix[rows, :] = dot_nt(cot[rows, :], w_out[...]).astype(bf16)
    out3[...] = dot(hot_t[R:K, :], gmix[...]).astype(bf16)
    exchange(1, out3, got3, 0)

    arrive("w_edge")
    inv[0:R, :] = 1.0 / (dot(hot_t[0:R, :], ones) + 1.0)
    means[0:R, :] = (dot(hot_t[0:R, :], msg[...]) * inv[0:R, 0:1]).astype(bf16)
    arrived(0, got1)
    counted = dot(tgt_t[...], got1[:, D:])
    inv[R:, :] = jnp.broadcast_to(
        1.0 / (counted[:, 0:1] + counted[:, S // 2 : S // 2 + 1] + 1.0), (H, S)
    )
    means[R:, :] = (dot(tgt_t[...], got1[:, 0:D]) * inv[R:, 0:1]).astype(bf16)
    hout[...] = dot(means[R:, :], w_edge[...]).astype(bf16)
    reply2[...] = dot_tn(tgt_t[...], hout[...]).astype(bf16)
    exchange(2, reply2, cat2, R)
    cat2[0:R, :] = dot(means[0:R, :], w_edge[...]).astype(bf16)
    hgrads[0:R, :] = dot(hot_t[0:R, :], gmix[...]).astype(bf16)
    arrived(1, got3)
    hgrads[R:, :] = dot(tgt_t[...], got3[...]).astype(bf16)
    gmean[...] = (dot_nt(hgrads[R:, :], w_edge[...]) * inv[R:, 0:1]).astype(bf16)
    reply4[...] = dot_tn(tgt_t[...], gmean[...]).astype(bf16)
    exchange(3, reply4, cat4, R)
    cat4[0:R, :] = (dot_nt(hgrads[0:R, :], w_edge[...]) * inv[0:R, 0:1]).astype(bf16)

    near = pl.ds(aligned(core * HALF, 128), HALF)
    far = pl.ds(aligned((1 - core) * HALF, 128), HALF)
    axes = ((0, 1, 2), (1, 2, 0), (2, 0, 1))

    def piece_a(base, t, a):
        return (
            pl.ds(aligned(base + t * 128 + lax.div(a, 2) * 64, 64), 64),
            pl.ds(aligned(lax.rem(a, 2) * HALF, 128), HALF),
        )

    def piece_b(base, t, a, b):
        return (
            pl.ds(aligned(base + t * 128 + lax.div(a, 2) * 64 + b * 16, 16), 16),
            pl.ds(aligned(lax.rem(a, 2) * HALF, 128), HALF),
        )

    def around(ax, k):
        return lax.rem(at[ax] + k, 4)

    def some(span):
        return pl.ds(span[0], span[1])

    def gradient(g, left, right):
        send0[g] = dot_tn(left[:, far], right[...]).astype(bf16)
        send(send0.at[g], recv0.at[g], p_ss.at[g], p_rs.at[g], twin)
        sent.append((send0.at[g], p_ss.at[g]))
        part[g] = dot_tn(left[:, near], right[...])

    def step_a(span):
        gs, q = some(span), span[0]
        for g in range(span[0], span[0] + span[1]):
            take(recv0.at[g], p_rs.at[g])
            send_a[g] = (part[g] + recv0[g].astype(f32)).astype(bf16)
        for k in (2, 1, 3):
            for t in range(3):
                ax = axes[t][0]
                r, c = piece_a(0, t, around(ax, k))
                send(send_a.at[gs, r, c], recv_a.at[k - 1, t, gs], a_ss.at[q], a_rs.at[q], peer[ax](k))
        sent.append((recv_a.at[:, :, gs], a_ss.at[q]))

    def step_b(span):
        gs, q = some(span), span[0]
        take(recv_a.at[:, :, gs], a_rs.at[q])
        for t in range(3):
            ax = axes[t][1]
            r, c = piece_a(0, t, at[axes[t][0]])
            total = part[gs, r, c] + recv0[gs, r, c].astype(f32)
            for k in range(3):
                total = total + recv_a[k, t, gs].astype(f32)
            part_b[t, gs] = total
            send_b[t, gs] = total.astype(bf16)
            for k in (2, 1, 3):
                theirs = pl.ds(aligned(around(ax, k) * 16, 16), 16)
                send(send_b.at[t, gs, theirs], recv_b.at[k - 1, t, gs], b_ss.at[q], b_rs.at[q], peer[ax](k))
        sent.append((recv_b.at[:, :, gs], b_ss.at[q]))

    def step_c(span):
        gs, q = some(span), span[0]
        take(recv_b.at[:, :, gs], b_rs.at[q])
        for t in range(3):
            ax = axes[t][2]
            mine = pl.ds(aligned(at[axes[t][1]] * 16, 16), 16)
            total = part_b[t, gs, mine, :]
            for k in range(3):
                total = total + recv_b[k, t, gs].astype(f32)
            recv_c[pl.ds(at[ax], 1), t, gs] = total.astype(bf16)[None]
            block = recv_c.at[at[ax], t, gs]
            for k in (2, 1, 3):
                send(block, block, c_ss.at[q], c_rs.at[q], peer[ax](k))
        sent.append((recv_b.at[:, :, gs], c_ss.at[q]))

    def gather_b(span):
        gs, q = some(span), span[0]
        take(recv_b.at[:, :, gs], c_rs.at[q])
        for t in range(3):
            ax = axes[t][1]
            total = recv_c[0, t, gs].astype(f32)
            for k in (1, 2, 3):
                total = total + recv_c[k, t, gs].astype(f32)
            r, c = piece_b(core * HALF, t, at[axes[t][0]], at[ax])
            fin[gs, r, c] = total.astype(bf16)
            block = fin.at[gs, r, c]
            for k in (2, 1, 3):
                send(block, block, bg_ss.at[q], bg_rs.at[q], peer[ax](k))
        sent.append((recv_b.at[:, :, gs], bg_ss.at[q]))

    def gather_a(span):
        gs, q = some(span), span[0]
        take(recv_b.at[:, :, gs], bg_rs.at[q])
        for t in range(3):
            ax = axes[t][0]
            r, c = piece_a(core * HALF, t, at[ax])
            block = fin.at[gs, r, c]
            for k in (2, 1, 3):
                send(block, block, ag_ss.at[q], ag_rs.at[q], peer[ax](k))
        sent.append((recv_a.at[:, :, gs], ag_ss.at[q]))

    def gather_p(span):
        gs, q = some(span), span[0]
        take(recv_a.at[:, :, gs], ag_rs.at[q])
        block = fin.at[gs, near]
        send(block, block, pg_ss.at[q], pg_rs.at[q], twin)
        sent.append((block, pg_ss.at[q]))

    def all_sent():
        for ref, sem in sent:
            take(ref, sem)
        sent.clear()

    def finish(span, *outs):
        for g, out in enumerate(outs, span[0]):
            out[near, :] = fin[g, near, :].astype(f32)
        take(fin.at[some(span), far], pg_rs.at[span[0]])
        for g, out in enumerate(outs, span[0]):
            out[far, :] = fin[g, far, :].astype(f32)

    gradient(WEDGE, means, hgrads)
    arrived(2, cat2)
    for i in range(N // M):
        rows = pl.ds(i * M, M)
        mixed[rows, :] = dot(hot[rows, :], cat2[...]).astype(bf16)
    gradient(WOUT, mixed, cot)
    arrived(3, cat4)
    for i in range(N // M):
        rows = pl.ds(i * M, M)
        gpre[rows, :] = (dot(hot[rows, :], cat4[...]) * dact[rows, :].astype(f32)).astype(bf16)
    step_a(BOTH)
    gradient(WIN, cells, gpre)
    step_a(LAST)

    def layer_out(i):
        rows = pl.ds(i * M, M)
        mixed[rows, :] = (cells[rows, :].astype(f32) + dot(mixed[rows, :], w_out[...])).astype(bf16)

    def grad_cells(i):
        rows = pl.ds(i * M, M)
        gpre[rows, :] = (cot[rows, :].astype(f32) + dot_nt(gpre[rows, :], w_in[...])).astype(bf16)

    layer_out(0)
    step_b(BOTH)
    layer_out(1)
    step_b(LAST)
    step_c(BOTH)
    grad_cells(0)
    step_c(LAST)
    gather_b(BOTH)
    grad_cells(1)
    gather_b(LAST)
    gather_a(BOTH)
    gather_a(LAST)
    all_sent()
    gather_p(BOTH)
    gather_p(LAST)
    finish(BOTH, wedge_ref, wout_ref)
    finish(LAST, win_ref)
    all_sent()


def write(*refs):
    n = len(refs) // 2
    copies = [
        pltpu.make_async_copy(refs[i], refs[n + i], refs[2 * n].at[i]) for i in range(n)
    ]
    for copy in copies:
        copy.start()
    for copy in copies:
        copy.wait()


def per_device(cells_in, w_in, w_edge, w_out, cotangent, cell_row, send_slot, recv_target):
    any_spec = pl.BlockSpec(memory_space=pl.ANY)
    vmem = pl.BlockSpec(memory_space=pltpu.VMEM)
    dma = pltpu.SemaphoreType.DMA
    scratch = [
        pltpu.VMEM((1, N), jnp.int32),
        pltpu.VMEM((2, N), jnp.int32),
        pltpu.VMEM((1, S), jnp.int32),
        pltpu.VMEM((N, D), bf16),
        pltpu.VMEM((N, D), bf16),
        pltpu.VMEM((D, D), bf16),
        pltpu.VMEM((D, D), bf16),
        pltpu.VMEM((D, D), bf16),
        pltpu.VMEM((N, D), bf16),
        pltpu.VMEM((K, N), bf16),
        pltpu.VMEM((N, K), bf16),
        pltpu.VMEM((8, N), jnp.int32),
        pltpu.VMEM((R + H, D), bf16),
        pltpu.VMEM((R + H, D), bf16),
        pltpu.VMEM((H, D), bf16),
        pltpu.VMEM((H, D), bf16),
        pltpu.VMEM((H, S), bf16),
        pltpu.VMEM((R + H, S), f32),
        pltpu.VMEM((S, D + S), bf16),
        pltpu.VMEM((S, D), bf16),
        pltpu.VMEM((S, D + S), bf16),
        pltpu.VMEM((S, D), bf16),
        pltpu.VMEM((S, D), bf16),
        pltpu.VMEM((S, D), bf16),
        pltpu.VMEM((K, D), bf16),
        pltpu.VMEM((K, D), bf16),
        pltpu.VMEM((3, HALF, D), bf16),
        pltpu.VMEM((3, HALF, D), bf16),
        pltpu.VMEM((3, HALF, D), f32),
        pltpu.VMEM((3, HALF, D), bf16),
        pltpu.VMEM((3, 3, 3, 64, HALF), bf16),
        pltpu.VMEM((3, 3, 64, HALF), f32),
        pltpu.VMEM((3, 3, 64, HALF), bf16),
        pltpu.VMEM((3, 3, 3, 16, HALF), bf16),
        pltpu.VMEM((4, 3, 3, 16, HALF), bf16),
        pltpu.VMEM((3, D, D), bf16),
        dma((10,)),
        dma((4,)),
        dma((4,)),
        dma((3,)),
        dma((3,)),
        dma((3,)),
        dma((3,)),
        dma((3,)),
        dma((3,)),
        dma((3,)),
        dma((3,)),
        dma((3,)),
        dma((3,)),
        dma((3,)),
        dma((3,)),
        dma((3,)),
        dma((3,)),
    ]
    results = pl.pallas_call(
        kernel,
        out_shape=(
            pltpu.VMEM((N, D), bf16),
            pltpu.VMEM((N, D), bf16),
            pltpu.VMEM((D, D), f32),
            pltpu.VMEM((D, D), f32),
            pltpu.VMEM((D, D), f32),
        ),
        in_specs=[any_spec] * 8,
        out_specs=[vmem] * 5,
        scratch_shapes=scratch,
        compiler_params=pltpu.CompilerParams(
            collective_id=0, has_side_effects=True, vmem_limit_bytes=44 * 2**20
        ),
        name="layer",
    )(
        cells_in, w_in, w_edge, w_out, cotangent,
        cell_row.reshape(1, N), send_slot, recv_target,
    )
    outs = tuple(jax.ShapeDtypeStruct(r.shape, r.dtype) for r in results)
    return pl.pallas_call(
        write,
        out_shape=outs,
        in_specs=[any_spec] * 5,
        out_specs=[any_spec] * 5,
        scratch_shapes=[dma((5,))],
        compiler_params=pltpu.CompilerParams(vmem_limit_bytes=2**20),
        name="write",
    )(*results)


def solution(mesh):
    placed = (
        P(("cells", "edges"), None),
        P(),
        P(),
        P(),
        P(("cells", "edges"), None),
        P(("cells", "edges")),
        P(None, ("cells", "edges")),
        P(("cells", "edges"), None),
    )
    return jax.shard_map(
        per_device,
        mesh=mesh,
        in_specs=placed,
        out_specs=(P(("cells", "edges"), None), P(("cells", "edges"), None), P(), P(), P()),
        check_vma=False,
    )
```

time: 80.1 us -> 65.2 us (0.81)
  local copies, waits for them, and re-layouts: 8.47 us -> 0 us
  Pallas kernels: 68.1 us -> 64.2 us
  other arithmetic: 2.6 us -> 0 us
    unnamed x6 -> x0, local copies, waits for them, and re-layouts: 5.1 us -> none
    pallas_call x1 -> x2, Pallas kernels: 68.1 us -> 64.2 us  [the longest x1 59.3 us: per_device(): pl.pallas_call(kernel, out_shape=(pltpu.VMEM((N, D), bf16), pltpu.VMEM((N...]
    squeeze x1 -> x0, local copies, waits for them, and re-layouts: 3.37 us -> none  [per_device(): return (layer_out, grad_cells, wide[WIN], wide[WEDGE], wide[WOUT])]
    convert_element_type x1 -> x0, other arithmetic: 2.6 us -> none  [per_device(): wide = fin.astype(f32)]
where the time goes in v2:
time: 65.2 us; the launch traced here: 65 us
  Pallas kernels  64.2 us (98%)
  between operations  0.8 us (1%)
    pallas_call x1, Pallas kernels, per_device(): pl.pallas_call(kernel, out_shape=(pltpu.VMEM((N, D), bf16), pltpu.VMEM((N...  59.3 us
    pallas_call x1, Pallas kernels, per_device(): pl.pallas_call(write, out_shape=outs, in_specs=[any_spec] * 5, out_specs=...  4.94 us

profile of v2, /device:TPU:1, one launch (start us, length us, event | category | flops | bytes accessed | tf_op | source)
XLA Modules:
  0.0 65.0 jit_solution(11819611606132150737)
XLA Ops:
  0.6 59.3 %layer.1 = (bf16[2048,768]{1,0:T(8,128)(2,1)S(1)}, bf16[2048,768]{1,0:T(8,128)(2,1)S(1)}, f32[768,768]{1,0:T(8,128)S(1)}, f32[768,768]{1,0:T(8,128)S(1)}, f32[768,768]{1,0:T(8,128)S(1)}) custom-call(bf16[2048,768]{1,0:T(8,128)(2,1)} %cells_h.1, bf16[768,768]{1,0:T(8,128)(2,1)} %w_in_h.1, bf16[768,768]{1,0:T(8,128)(2,1)} %w_edge_h.1, ...), custom_call_target="tpu_custom_call" | custom-call | tf_op jit(solution)/shard_map/layer/pallas_call | solution.py:440
  59.9 4.9 %write.1 = (bf16[2048,768]{1,0:T(8,128)(2,1)}, bf16[2048,768]{1,0:T(8,128)(2,1)}, f32[768,768]{1,0:T(8,128)}, f32[768,768]{1,0:T(8,128)}, f32[768,768]{1,0:T(8,128)}) custom-call(bf16[2048,768]{1,0:T(8,128)(2,1)S(1)} %get-tuple-element.10.refs_0_, bf16[2048,768]{1,0:T(8,128)(2,1)S(1)} %get-tuple-element.11.refs_1_, ...), custom_call_target="tpu_custom_call" | custom-call | tf_op jit(solution)/shard_map/write/pallas_call | solution.py:461

commit v3 on v2

--- a/solution.py
+++ b/solution.py
@@ -43,7 +43,7 @@
 def kernel(
     cells_h, w_in_h, w_edge_h, w_out_h, cot_h, row_h, slot_h, tgt_h,
     mixed, gpre, win_ref, wedge_ref, wout_ref,
-    row_ref, slot_ref, tgt_ref, cells, cot, w_in, w_edge, w_out, dact, hot_t, hot, ids,
+    row_ref, slot_ref, tgt_ref, cells, cot, w_in, w_edge, w_out, dact, hot_t,
     means, hgrads, hout, gmean, tgt_t, inv,
     out1, out3, got1, got3, reply2, reply4, cat2, cat4,
     send0, recv0, part, send_a, recv_a, part_b, send_b, recv_b, recv_c, fin,
@@ -118,34 +118,18 @@
 
     for name in ("rows", "slots", "targets"):
         arrive(name)
-    ids[...] = jnp.zeros_like(ids)
-    ids[0:1, :] = row_ref[...]
-    ids[1:3, :] = slot_ref[...]
     tgt_t[...] = (lax.broadcasted_iota(jnp.int32, (H, S), 0) == tgt_ref[...]).astype(bf16)
 
     def ones_where(mask):
         return jnp.where(mask, 1.0, 0.0)
 
-    def incidences(i):
-        rows = pl.ds(i * M, M)
-        some = ids[:, rows]
-        hot_t[0:R, rows] = ones_where(
-            lax.broadcasted_iota(jnp.int32, (R, M), 0) == some[0:1, :]
-        ).astype(bf16)
-        slot_i = lax.broadcasted_iota(jnp.int32, (S, M), 0)
-        hot_t[R:K, rows] = (
-            ones_where(slot_i == some[1:2, :]) + ones_where(slot_i == some[2:3, :])
-        ).astype(bf16)
-        col = some.T
-        hot[rows, 0:R] = ones_where(
-            lax.broadcasted_iota(jnp.int32, (M, R), 1) == col[:, 0:1]
-        ).astype(bf16)
-        slot_j = lax.broadcasted_iota(jnp.int32, (M, S), 1)
-        hot[rows, R:K] = (
-            ones_where(slot_j == col[:, 1:2]) + ones_where(slot_j == col[:, 2:3])
-        ).astype(bf16)
-
-    incidences(0)
+    hot_t[0:R, :] = ones_where(
+        lax.broadcasted_iota(jnp.int32, (R, N), 0) == row_ref[...]
+    ).astype(bf16)
+    slot_i = lax.broadcasted_iota(jnp.int32, (S, N), 0)
+    hot_t[R:K, :] = (
+        ones_where(slot_i == slot_ref[0:1, :]) + ones_where(slot_i == slot_ref[1:2, :])
+    ).astype(bf16)
     arrive("w_in")
     for i in range(N // M):
         rows = pl.ds(i * M, M)
@@ -155,8 +139,6 @@
         m = pre * sig
         msg[rows, :] = m.astype(bf16)
         dact[rows, :] = (sig + m * (1.0 - sig)).astype(bf16)
-        if i == 0:
-            incidences(1)
 
     ones = jnp.ones((N, S), bf16)
     out1[:, 0:D] = dot(hot_t[R:K, :], msg[...]).astype(bf16)
@@ -177,37 +159,6 @@
 
     def arrived(kind, dst):
         take(dst.at[pl.ds(0, 3 * CAP)], x_rs.at[kind])
-
-    exchange(0, out1, got1, 0)
-
-    arrive("w_out")
-    for i in range(N // M):
-        rows = pl.ds(i * M, M)
-        arrive("cot%d" % i)
-        gmix[rows, :] = dot_nt(cot[rows, :], w_out[...]).astype(bf16)
-    out3[...] = dot(hot_t[R:K, :], gmix[...]).astype(bf16)
-    exchange(1, out3, got3, 0)
-
-    arrive("w_edge")
-    inv[0:R, :] = 1.0 / (dot(hot_t[0:R, :], ones) + 1.0)
-    means[0:R, :] = (dot(hot_t[0:R, :], msg[...]) * inv[0:R, 0:1]).astype(bf16)
-    arrived(0, got1)
-    counted = dot(tgt_t[...], got1[:, D:])
-    inv[R:, :] = jnp.broadcast_to(
-        1.0 / (counted[:, 0:1] + counted[:, S // 2 : S // 2 + 1] + 1.0), (H, S)
-    )
-    means[R:, :] = (dot(tgt_t[...], got1[:, 0:D]) * inv[R:, 0:1]).astype(bf16)
-    hout[...] = dot(means[R:, :], w_edge[...]).astype(bf16)
-    reply2[...] = dot_tn(tgt_t[...], hout[...]).astype(bf16)
-    exchange(2, reply2, cat2, R)
-    cat2[0:R, :] = dot(means[0:R, :], w_edge[...]).astype(bf16)
-    hgrads[0:R, :] = dot(hot_t[0:R, :], gmix[...]).astype(bf16)
-    arrived(1, got3)
-    hgrads[R:, :] = dot(tgt_t[...], got3[...]).astype(bf16)
-    gmean[...] = (dot_nt(hgrads[R:, :], w_edge[...]) * inv[R:, 0:1]).astype(bf16)
-    reply4[...] = dot_tn(tgt_t[...], gmean[...]).astype(bf16)
-    exchange(3, reply4, cat4, R)
-    cat4[0:R, :] = (dot_nt(hgrads[0:R, :], w_edge[...]) * inv[0:R, 0:1]).astype(bf16)
 
     near = pl.ds(aligned(core * HALF, 128), HALF)
     far = pl.ds(aligned((1 - core) * HALF, 128), HALF)
@@ -295,47 +246,87 @@
                 send(block, block, bg_ss.at[q], bg_rs.at[q], peer[ax](k))
         sent.append((recv_b.at[:, :, gs], bg_ss.at[q]))
 
+    def to_twin(span, t, a):
+        r, c = piece_a(core * HALF, t, a)
+        block = fin.at[some(span), r, c]
+        send(block, block, pg_ss.at[span[0]], pg_rs.at[span[0]], twin)
+
     def gather_a(span):
         gs, q = some(span), span[0]
         take(recv_b.at[:, :, gs], bg_rs.at[q])
+        for k in (1, 3, 2):
+            for t in range(3):
+                ax = axes[t][0]
+                r, c = piece_a(core * HALF, t, at[ax])
+                block = fin.at[gs, r, c]
+                send(block, block, ag_ss.at[q], ag_rs.at[q, k - 1], peer[ax](k))
+        sent.append((recv_a.at[:, :, gs], ag_ss.at[q]))
         for t in range(3):
-            ax = axes[t][0]
-            r, c = piece_a(core * HALF, t, at[ax])
-            block = fin.at[gs, r, c]
-            for k in (2, 1, 3):
-                send(block, block, ag_ss.at[q], ag_rs.at[q], peer[ax](k))
-        sent.append((recv_a.at[:, :, gs], ag_ss.at[q]))
-
-    def gather_p(span):
-        gs, q = some(span), span[0]
-        take(recv_a.at[:, :, gs], ag_rs.at[q])
-        block = fin.at[gs, near]
-        send(block, block, pg_ss.at[q], pg_rs.at[q], twin)
-        sent.append((block, pg_ss.at[q]))
+            to_twin(span, t, at[axes[t][0]])
+        sent.append((fin.at[gs, near], pg_ss.at[q]))
+
+    def gather_p(span, k):
+        take(recv_a.at[k - 1, :, some(span)], ag_rs.at[span[0], k - 1])
+        for t in range(3):
+            to_twin(span, t, around(axes[t][0], 4 - k))
 
     def all_sent():
         for ref, sem in sent:
             take(ref, sem)
         sent.clear()
 
-    def finish(span, *outs):
+    def finish_near(span, *outs):
         for g, out in enumerate(outs, span[0]):
             out[near, :] = fin[g, near, :].astype(f32)
+
+    def finish_far(span, *outs):
         take(fin.at[some(span), far], pg_rs.at[span[0]])
         for g, out in enumerate(outs, span[0]):
             out[far, :] = fin[g, far, :].astype(f32)
 
-    gradient(WEDGE, means, hgrads)
+    def grad_mixed(i):
+        rows = pl.ds(i * M, M)
+        arrive("cot%d" % i)
+        gmix[rows, :] = dot_nt(cot[rows, :], w_out[...]).astype(bf16)
+
+    exchange(0, out1, got1, 0)
+    inv[0:R, :] = 1.0 / (dot(hot_t[0:R, :], ones) + 1.0)
+    means[0:R, :] = (dot(hot_t[0:R, :], msg[...]) * inv[0:R, 0:1]).astype(bf16)
+    arrive("w_out")
+    grad_mixed(0)
+    arrive("w_edge")
+    arrived(0, got1)
+    counted = dot(tgt_t[...], got1[:, D:])
+    inv[R:, :] = jnp.broadcast_to(
+        1.0 / (counted[:, 0:1] + counted[:, S // 2 : S // 2 + 1] + 1.0), (H, S)
+    )
+    means[R:, :] = (dot(tgt_t[...], got1[:, 0:D]) * inv[R:, 0:1]).astype(bf16)
+    hout[...] = dot(means[R:, :], w_edge[...]).astype(bf16)
+    reply2[...] = dot_tn(tgt_t[...], hout[...]).astype(bf16)
+    exchange(2, reply2, cat2, R)
+    grad_mixed(1)
+    out3[...] = dot(hot_t[R:K, :], gmix[...]).astype(bf16)
+    exchange(1, out3, got3, 0)
+    cat2[0:R, :] = dot(means[0:R, :], w_edge[...]).astype(bf16)
     arrived(2, cat2)
     for i in range(N // M):
         rows = pl.ds(i * M, M)
-        mixed[rows, :] = dot(hot[rows, :], cat2[...]).astype(bf16)
+        mixed[rows, :] = dot_tn(hot_t[:, rows], cat2[...]).astype(bf16)
     gradient(WOUT, mixed, cot)
+    arrived(1, got3)
+    hgrads[R:, :] = dot(tgt_t[...], got3[...]).astype(bf16)
+    gmean[...] = (dot_nt(hgrads[R:, :], w_edge[...]) * inv[R:, 0:1]).astype(bf16)
+    reply4[...] = dot_tn(tgt_t[...], gmean[...]).astype(bf16)
+    exchange(3, reply4, cat4, R)
+    hgrads[0:R, :] = dot(hot_t[0:R, :], gmix[...]).astype(bf16)
+    cat4[0:R, :] = (dot_nt(hgrads[0:R, :], w_edge[...]) * inv[0:R, 0:1]).astype(bf16)
+    gradient(WEDGE, means, hgrads)
     arrived(3, cat4)
     for i in range(N // M):
         rows = pl.ds(i * M, M)
-        gpre[rows, :] = (dot(hot[rows, :], cat4[...]) * dact[rows, :].astype(f32)).astype(bf16)
-    step_a(BOTH)
+        gpre[rows, :] = (dot_tn(hot_t[:, rows], cat4[...]) * dact[rows, :].astype(f32)).astype(bf16)
+        if i == 0:
+            step_a(BOTH)
     gradient(WIN, cells, gpre)
     step_a(LAST)
 
@@ -343,27 +334,31 @@
         rows = pl.ds(i * M, M)
         mixed[rows, :] = (cells[rows, :].astype(f32) + dot(mixed[rows, :], w_out[...])).astype(bf16)
 
-    def grad_cells(i):
-        rows = pl.ds(i * M, M)
+    def grad_cells(start, n):
+        rows = pl.ds(start, n)
         gpre[rows, :] = (cot[rows, :].astype(f32) + dot_nt(gpre[rows, :], w_in[...])).astype(bf16)
 
     layer_out(0)
     step_b(BOTH)
     layer_out(1)
     step_b(LAST)
+    grad_cells(0, M)
     step_c(BOTH)
-    grad_cells(0)
+    grad_cells(M, M // 2)
     step_c(LAST)
+    grad_cells(M + M // 2, M // 2)
+    all_sent()
     gather_b(BOTH)
-    grad_cells(1)
     gather_b(LAST)
     gather_a(BOTH)
     gather_a(LAST)
-    all_sent()
-    gather_p(BOTH)
-    gather_p(LAST)
-    finish(BOTH, wedge_ref, wout_ref)
-    finish(LAST, win_ref)
+    for span in (BOTH, LAST):
+        for k in (1, 3, 2):
+            gather_p(span, k)
+    finish_near(BOTH, wedge_ref, wout_ref)
+    finish_near(LAST, win_ref)
+    finish_far(BOTH, wedge_ref, wout_ref)
+    finish_far(LAST, win_ref)
     all_sent()
 
 
@@ -393,8 +388,6 @@
         pltpu.VMEM((D, D), bf16),
         pltpu.VMEM((N, D), bf16),
         pltpu.VMEM((K, N), bf16),
-        pltpu.VMEM((N, K), bf16),
-        pltpu.VMEM((8, N), jnp.int32),
         pltpu.VMEM((R + H, D), bf16),
         pltpu.VMEM((R + H, D), bf16),
         pltpu.VMEM((H, D), bf16),
@@ -433,7 +426,7 @@
         dma((3,)),
         dma((3,)),
         dma((3,)),
-        dma((3,)),
+        dma((3, 3)),
         dma((3,)),
         dma((3,)),
     ]

time: 65.2 us -> 70 us (1.074)
  Pallas kernels: 64.2 us -> 69 us
    pallas_call x1, Pallas kernels: 59.3 us -> 64.1 us  [per_device(): pl.pallas_call(kernel, out_shape=(pltpu.VMEM((N, D), bf16), pltpu.VMEM((N...]
where the time goes in v3:
time: 70 us; the launch traced here: 69.8 us
  Pallas kernels  69 us (99%)
  between operations  0.82 us (1%)
    pallas_call x1, Pallas kernels, per_device(): pl.pallas_call(kernel, out_shape=(pltpu.VMEM((N, D), bf16), pltpu.VMEM((N...  64.1 us
    pallas_call x1, Pallas kernels, per_device(): pl.pallas_call(write, out_shape=outs, in_specs=[any_spec] * 5, out_specs=...  4.94 us

profile of v3, /device:TPU:1, one launch (start us, length us, event | category | flops | bytes accessed | tf_op | source)
XLA Modules:
  0.0 69.8 jit_solution(16612715885936649029)
XLA Ops:
  0.6 64.1 %layer.1 = (bf16[2048,768]{1,0:T(8,128)(2,1)S(1)}, bf16[2048,768]{1,0:T(8,128)(2,1)S(1)}, f32[768,768]{1,0:T(8,128)S(1)}, f32[768,768]{1,0:T(8,128)S(1)}, f32[768,768]{1,0:T(8,128)S(1)}) custom-call(bf16[2048,768]{1,0:T(8,128)(2,1)} %cells_h.1, bf16[768,768]{1,0:T(8,128)(2,1)} %w_in_h.1, bf16[768,768]{1,0:T(8,128)(2,1)} %w_edge_h.1, ...), custom_call_target="tpu_custom_call" | custom-call | tf_op jit(solution)/shard_map/layer/pallas_call | solution.py:433
  64.7 4.9 %write.1 = (bf16[2048,768]{1,0:T(8,128)(2,1)}, bf16[2048,768]{1,0:T(8,128)(2,1)}, f32[768,768]{1,0:T(8,128)}, f32[768,768]{1,0:T(8,128)}, f32[768,768]{1,0:T(8,128)}) custom-call(bf16[2048,768]{1,0:T(8,128)(2,1)S(1)} %get-tuple-element.10.refs_0_, bf16[2048,768]{1,0:T(8,128)(2,1)S(1)} %get-tuple-element.11.refs_1_, ...), custom_call_target="tpu_custom_call" | custom-call | tf_op jit(solution)/shard_map/write/pallas_call | solution.py:454

commit v4 on v3

--- a/solution.py
+++ b/solution.py
@@ -290,11 +290,14 @@
         gmix[rows, :] = dot_nt(cot[rows, :], w_out[...]).astype(bf16)
 
     exchange(0, out1, got1, 0)
+    arrive("w_out")
+    grad_mixed(0)
+    grad_mixed(1)
+    out3[...] = dot(hot_t[R:K, :], gmix[...]).astype(bf16)
+    exchange(1, out3, got3, 0)
+    arrive("w_edge")
     inv[0:R, :] = 1.0 / (dot(hot_t[0:R, :], ones) + 1.0)
     means[0:R, :] = (dot(hot_t[0:R, :], msg[...]) * inv[0:R, 0:1]).astype(bf16)
-    arrive("w_out")
-    grad_mixed(0)
-    arrive("w_edge")
     arrived(0, got1)
     counted = dot(tgt_t[...], got1[:, D:])
     inv[R:, :] = jnp.broadcast_to(
@@ -304,29 +307,25 @@
     hout[...] = dot(means[R:, :], w_edge[...]).astype(bf16)
     reply2[...] = dot_tn(tgt_t[...], hout[...]).astype(bf16)
     exchange(2, reply2, cat2, R)
-    grad_mixed(1)
-    out3[...] = dot(hot_t[R:K, :], gmix[...]).astype(bf16)
-    exchange(1, out3, got3, 0)
     cat2[0:R, :] = dot(means[0:R, :], w_edge[...]).astype(bf16)
+    hgrads[0:R, :] = dot(hot_t[0:R, :], gmix[...]).astype(bf16)
+    arrived(1, got3)
+    hgrads[R:, :] = dot(tgt_t[...], got3[...]).astype(bf16)
+    gmean[...] = (dot_nt(hgrads[R:, :], w_edge[...]) * inv[R:, 0:1]).astype(bf16)
+    reply4[...] = dot_tn(tgt_t[...], gmean[...]).astype(bf16)
+    exchange(3, reply4, cat4, R)
+    cat4[0:R, :] = (dot_nt(hgrads[0:R, :], w_edge[...]) * inv[0:R, 0:1]).astype(bf16)
+    gradient(WEDGE, means, hgrads)
     arrived(2, cat2)
     for i in range(N // M):
         rows = pl.ds(i * M, M)
         mixed[rows, :] = dot_tn(hot_t[:, rows], cat2[...]).astype(bf16)
     gradient(WOUT, mixed, cot)
-    arrived(1, got3)
-    hgrads[R:, :] = dot(tgt_t[...], got3[...]).astype(bf16)
-    gmean[...] = (dot_nt(hgrads[R:, :], w_edge[...]) * inv[R:, 0:1]).astype(bf16)
-    reply4[...] = dot_tn(tgt_t[...], gmean[...]).astype(bf16)
-    exchange(3, reply4, cat4, R)
-    hgrads[0:R, :] = dot(hot_t[0:R, :], gmix[...]).astype(bf16)
-    cat4[0:R, :] = (dot_nt(hgrads[0:R, :], w_edge[...]) * inv[0:R, 0:1]).astype(bf16)
-    gradient(WEDGE, means, hgrads)
     arrived(3, cat4)
     for i in range(N // M):
         rows = pl.ds(i * M, M)
         gpre[rows, :] = (dot_tn(hot_t[:, rows], cat4[...]) * dact[rows, :].astype(f32)).astype(bf16)
-        if i == 0:
-            step_a(BOTH)
+    step_a(BOTH)
     gradient(WIN, cells, gpre)
     step_a(LAST)
 

time: 70 us -> 64.9 us (0.927)
  Pallas kernels: 69 us -> 64 us
    pallas_call x1, Pallas kernels: 64.1 us -> 59 us  [per_device(): pl.pallas_call(kernel, out_shape=(pltpu.VMEM((N, D), bf16), pltpu.VMEM((N...]
where the time goes in v4:
time: 64.9 us; the launch traced here: 64.8 us
  Pallas kernels  64 us (99%)
  between operations  0.8 us (1%)
    pallas_call x1, Pallas kernels, per_device(): pl.pallas_call(kernel, out_shape=(pltpu.VMEM((N, D), bf16), pltpu.VMEM((N...  59 us
    pallas_call x1, Pallas kernels, per_device(): pl.pallas_call(write, out_shape=outs, in_specs=[any_spec] * 5, out_specs=...  4.94 us

profile of v4, /device:TPU:1, one launch (start us, length us, event | category | flops | bytes accessed | tf_op | source)
XLA Modules:
  0.0 64.8 jit_solution(17711305877951706921)
XLA Ops:
  0.6 59.0 %layer.1 = (bf16[2048,768]{1,0:T(8,128)(2,1)S(1)}, bf16[2048,768]{1,0:T(8,128)(2,1)S(1)}, f32[768,768]{1,0:T(8,128)S(1)}, f32[768,768]{1,0:T(8,128)S(1)}, f32[768,768]{1,0:T(8,128)S(1)}) custom-call(bf16[2048,768]{1,0:T(8,128)(2,1)} %cells_h.1, bf16[768,768]{1,0:T(8,128)(2,1)} %w_in_h.1, bf16[768,768]{1,0:T(8,128)(2,1)} %w_edge_h.1, ...), custom_call_target="tpu_custom_call" | custom-call | tf_op jit(solution)/shard_map/layer/pallas_call | solution.py:432
  59.7 4.9 %write.1 = (bf16[2048,768]{1,0:T(8,128)(2,1)}, bf16[2048,768]{1,0:T(8,128)(2,1)}, f32[768,768]{1,0:T(8,128)}, f32[768,768]{1,0:T(8,128)}, f32[768,768]{1,0:T(8,128)}) custom-call(bf16[2048,768]{1,0:T(8,128)(2,1)S(1)} %get-tuple-element.10.refs_0_, bf16[2048,768]{1,0:T(8,128)(2,1)S(1)} %get-tuple-element.11.refs_1_, ...), custom_call_target="tpu_custom_call" | custom-call | tf_op jit(solution)/shard_map/write/pallas_call | solution.py:453

commit v5 on v4

--- a/solution.py
+++ b/solution.py
@@ -130,6 +130,12 @@
     hot_t[R:K, :] = (
         ones_where(slot_i == slot_ref[0:1, :]) + ones_where(slot_i == slot_ref[1:2, :])
     ).astype(bf16)
+    ones = jnp.ones((N, S), bf16)
+    inv[0:R, :] = 1.0 / (dot(hot_t[0:R, :], ones) + 1.0)
+    count = dot(hot_t[R:K, :], ones)
+    high = jnp.floor(count * (1.0 / 128.0)) * 128.0
+    lane = lax.broadcasted_iota(jnp.int32, (S, S), 1)
+    out1[:, D:] = jnp.where(lane < S // 2, high, count - high).astype(bf16)
     arrive("w_in")
     for i in range(N // M):
         rows = pl.ds(i * M, M)
@@ -140,13 +146,7 @@
         msg[rows, :] = m.astype(bf16)
         dact[rows, :] = (sig + m * (1.0 - sig)).astype(bf16)
 
-    ones = jnp.ones((N, S), bf16)
     out1[:, 0:D] = dot(hot_t[R:K, :], msg[...]).astype(bf16)
-    count = dot(hot_t[R:K, :], ones)
-    high = jnp.floor(count * (1.0 / 128.0)) * 128.0
-    lane = lax.broadcasted_iota(jnp.int32, (S, S), 1)
-    out1[:, D:] = jnp.where(lane < S // 2, high, count - high).astype(bf16)
-
     pl.semaphore_wait(barrier, 10)
 
     def exchange(kind, src, dst, base):
@@ -296,7 +296,6 @@
     out3[...] = dot(hot_t[R:K, :], gmix[...]).astype(bf16)
     exchange(1, out3, got3, 0)
     arrive("w_edge")
-    inv[0:R, :] = 1.0 / (dot(hot_t[0:R, :], ones) + 1.0)
     means[0:R, :] = (dot(hot_t[0:R, :], msg[...]) * inv[0:R, 0:1]).astype(bf16)
     arrived(0, got1)
     counted = dot(tgt_t[...], got1[:, D:])

time: 64.9 us -> 64.6 us (level)
  no operation moved by 1% of the time
where the time goes in v5:
time: 64.6 us; the launch traced here: 64.4 us
  Pallas kernels  63.6 us (98%)
  between operations  0.8 us (1%)
    pallas_call x1, Pallas kernels, per_device(): pl.pallas_call(kernel, out_shape=(pltpu.VMEM((N, D), bf16), pltpu.VMEM((N...  58.7 us
    pallas_call x1, Pallas kernels, per_device(): pl.pallas_call(write, out_shape=outs, in_specs=[any_spec] * 5, out_specs=...  4.94 us

profile of v5, /device:TPU:1, one launch (start us, length us, event | category | flops | bytes accessed | tf_op | source)
XLA Modules:
  0.0 64.4 jit_solution(12331927489379478604)
XLA Ops:
  0.6 58.7 %layer.1 = (bf16[2048,768]{1,0:T(8,128)(2,1)S(1)}, bf16[2048,768]{1,0:T(8,128)(2,1)S(1)}, f32[768,768]{1,0:T(8,128)S(1)}, f32[768,768]{1,0:T(8,128)S(1)}, f32[768,768]{1,0:T(8,128)S(1)}) custom-call(bf16[2048,768]{1,0:T(8,128)(2,1)} %cells_h.1, bf16[768,768]{1,0:T(8,128)(2,1)} %w_in_h.1, bf16[768,768]{1,0:T(8,128)(2,1)} %w_edge_h.1, ...), custom_call_target="tpu_custom_call" | custom-call | tf_op jit(solution)/shard_map/layer/pallas_call | solution.py:431
  59.3 4.9 %write.1 = (bf16[2048,768]{1,0:T(8,128)(2,1)}, bf16[2048,768]{1,0:T(8,128)(2,1)}, f32[768,768]{1,0:T(8,128)}, f32[768,768]{1,0:T(8,128)}, f32[768,768]{1,0:T(8,128)}) custom-call(bf16[2048,768]{1,0:T(8,128)(2,1)S(1)} %get-tuple-element.10.refs_0_, bf16[2048,768]{1,0:T(8,128)(2,1)S(1)} %get-tuple-element.11.refs_1_, ...), custom_call_target="tpu_custom_call" | custom-call | tf_op jit(solution)/shard_map/write/pallas_call | solution.py:452
